TPU v7x, 32 devices: a whole 2x2x4 slice. The times are simulated.
32 devices in a mesh: runs: 2 (over y), gy: 4 (over z), gx: 2 (over x), gz: 2 (over core).
Axes of the slice: x: 2, y: 2, z: 4, core: 2. Of those that a mesh axis runs over, the one named last changes fastest.
Arguments:
- box_state: float32 [8, 4, 2048, 256], P(None, 'gx', ('runs', 'gy'), 'gz'), parts along dimension 2, may hold values from -6 to 6
- shear_cells: int32 [4], P('runs'), parts along dimension 0, may hold values from 0 to 1023
- shear_fraction: float32 [4], P('runs'), parts along dimension 0, may hold values from 0 to 1
Outputs:
- advanced: float32 [8, 4, 2048, 256], P(None, 'gx', ('runs', 'gy'), 'gz'), parts along dimension 2
There are 2 independent parts, one for each index of `runs`. A program takes and returns all parts, laid end to end along the dimension named above; each array names one. Nothing has to cross between parts.
Inputs may be any that keep to these rules, and one draw needn't show every extreme that they name: `shear_cells`: whole cells of each section's azimuthal shear offset.
All inputs are finite; a program needn't handle non-finite values.
Results may differ from a plain program's by a relative error of at most 0.0003.
Values sent between devices are 32-bit elements; how exact they have to be, the bound alone decides.
A program may use at most 128 MiB of HBM per device.

v0:
```python
import functools
import math

import jax
import jax.numpy as jnp
from jax import lax
from jax.experimental import pallas as pl
from jax.experimental.pallas import tpu as pltpu
from jax.sharding import PartitionSpec as P

GHOST = 2

time_step = 0.25
sound_sq = 1.0
guide_field = 0.8
rotation = 1.0
shear_rate = 1.5
viscosity = 0.15
resistivity = 0.15
clean_sq = 1.0
damping_time = 2.0


MESH = pl.DeviceIdType.MESH
PAD = 8


def first_rows(rows, length, whole_cells, fraction, sign):
    j = lax.broadcasted_iota(jnp.int32, (rows, length), 1)
    m = lax.broadcasted_iota(jnp.int32, (rows, length), 0)
    q = jnp.mod(j - m + sign * whole_cells + length // 2, length) - length // 2
    x = q.astype(jnp.float32) + sign.astype(jnp.float32) * fraction
    parity = (1 - 2 * jnp.bitwise_and(q, 1)).astype(jnp.float32) * sign.astype(jnp.float32)
    sine = jnp.sin(math.pi * jnp.minimum(fraction, 1.0 - fraction))
    angle = (math.pi / length) * x
    near = jnp.abs(x) < 1e-5
    h = parity * (sine / length) * jnp.cos(angle) / jnp.where(near, 1.0, jnp.sin(angle))
    return jnp.where(near, 1.0, h)


def circulant(length, whole_cells, fraction, sign):
    rows = math.gcd(length, 128)
    block = first_rows(rows, length, whole_cells, fraction, sign)
    return jnp.concatenate(
        [jnp.roll(block, rows * b, axis=1) for b in range(length // rows)], axis=0
    )


def tile_rates(ref, r, row):
    length = ref.shape[3]

    def load(f, dr, dv):
        return ref[f, r + dr, pl.ds(row + dv, 8), :]

    centre, diff, one, two = [], [], [], []
    for f in range(8):
        c = load(f, 0, 0)
        near = [
            (load(f, 1, 0), load(f, -1, 0), load(f, 2, 0), load(f, -2, 0)),
            tuple(pltpu.roll(c, s % length, axis=1) for s in (-1, 1, -2, 2)),
            (load(f, 0, 1), load(f, 0, -1), load(f, 0, 2), load(f, 0, -2)),
        ]
        centre.append(c)
        diff.append([(2.0 / 3.0) * (n[0] - n[1]) - (1.0 / 12.0) * (n[2] - n[3]) for n in near])
        one.append(sum(n[0] + n[1] for n in near))
        two.append(sum(n[2] + n[3] for n in near))

    def d(f, dim):
        return diff[f][dim]

    def lap(f):
        return (4.0 / 3.0) * one[f] - (1.0 / 12.0) * two[f] - 7.5 * centre[f]

    flat = d(1, 0) + d(2, 1)
    return centre, [
        -(flat + d(3, 2)),
        -sound_sq * d(0, 0) + guide_field * (d(4, 2) - d(6, 0)) + 2.0 * rotation * centre[2] + viscosity * lap(1),
        -sound_sq * d(0, 1) + guide_field * (d(5, 2) - d(6, 1)) - (2.0 - shear_rate) * rotation * centre[1] + viscosity * lap(2),
        -sound_sq * d(0, 2) + viscosity * lap(3),
        guide_field * d(1, 2) - d(7, 0) + resistivity * lap(4),
        guide_field * d(2, 2) - shear_rate * rotation * centre[4] - d(7, 1) + resistivity * lap(5),
        -guide_field * flat - d(7, 2) + resistivity * lap(6),
        -clean_sq * (d(4, 0) + d(5, 1) + d(6, 2)) - (1.0 / damping_time) * centre[7],
    ]


def sections_kernel(gy, rows_ref, src, out, box, one, two, base, high, low,
                    z_send, z_recv, x_send, x_recv, own_sem, g_send, g_recv, g_own):
    me, x = lax.axis_index("gy"), lax.axis_index("gx")
    fields, radial, tall, azimuth = src.shape
    cells, length = 2 * radial, gy * azimuth
    wide = box.shape[2] - 2 * PAD
    part = wide - 4 * GHOST
    others = [lax.rem(me + s, gy) for s in range(gy)]
    sources = [lax.rem(me - s + gy, gy) for s in range(gy)]

    def clear(f, carry):
        edge = jnp.zeros((cells + 2 * GHOST, PAD, length), jnp.float32)
        for ref in (box, one):
            ref[f, :, :PAD, :] = edge
            ref[f, :, PAD + wide :, :] = edge
        return carry

    lax.fori_loop(0, fields, clear, 0)

    barrier = pltpu.get_barrier_semaphore()
    for s in range(1, gy):
        pl.semaphore_signal(barrier, inc=1, device_id={"gy": others[s]}, device_id_type=MESH)
    pl.semaphore_signal(barrier, inc=1, device_id={"gx": 1 - x}, device_id_type=MESH)
    pl.semaphore_wait(barrier, gy)

    def taken(p, target):
        return src.at[p, :, pl.ds(pl.multiple_of(target * part, 8), wide), :]

    def place(p, source, owner):
        return box.at[
            p,
            pl.ds(GHOST + owner * radial, radial),
            pl.ds(PAD, wide),
            pl.ds(pl.multiple_of(source * azimuth, 128), azimuth),
        ]

    def over_z(p, s):
        return pltpu.make_async_remote_copy(
            src_ref=taken(p, others[s]), dst_ref=place(p, me, x),
            send_sem=z_send.at[p, s], recv_sem=z_recv.at[p, s],
            device_id={"gy": others[s]}, device_id_type=MESH,
        )

    def z_landed(p, s):
        return pltpu.make_async_remote_copy(
            src_ref=taken(p, others[s]), dst_ref=place(p, sources[s], x),
            send_sem=z_send.at[p, s], recv_sem=z_recv.at[p, s],
            device_id={"gy": others[s]}, device_id_type=MESH,
        )

    def over_x(p, s):
        return pltpu.make_async_remote_copy(
            src_ref=taken(p, me) if s == 0 else place(p, sources[s], x),
            dst_ref=place(p, sources[s], x),
            send_sem=x_send.at[p, s], recv_sem=x_recv.at[p, s],
            device_id={"gx": 1 - x}, device_id_type=MESH,
        )

    def x_landed(p, s):
        return pltpu.make_async_remote_copy(
            src_ref=taken(p, me), dst_ref=place(p, sources[s], 1 - x),
            send_sem=x_send.at[p, s], recv_sem=x_recv.at[p, s],
            device_id={"gx": 1 - x}, device_id_type=MESH,
        )

    def kept(p):
        return pltpu.make_async_copy(taken(p, me), place(p, me, x), own_sem.at[p])

    def begin(p, carry):
        over_x(p, 0).start()
        for s in range(1, gy):
            over_z(p, s).start()
        kept(p).start()
        return carry

    lax.fori_loop(0, fields, begin, 0)

    def build(i):
        block = base.shape[0]
        for a in range(block // 8):
            base[8 * a : 8 * a + 8, :] = pltpu.roll(rows_ref[i], 8 * a, axis=1) if a else rows_ref[i]
        whole = base[...]
        coarse = whole.astype(jnp.bfloat16)
        fine = (whole - coarse.astype(jnp.float32)).astype(jnp.bfloat16)
        for b in range(length // block):
            for half, ref in ((coarse, high), (fine, low)):
                cut = length - block * b
                turned = jnp.concatenate([half[:, cut:], half[:, :cut]], axis=1) if b else half
                ref[i, block * b : block * (b + 1), :] = turned

    def move(ref, i, f, count, source, target):
        v = ref[pl.ds(f, count), pl.ds(source, GHOST), PAD : PAD + wide, :]
        v = v.reshape(count * GHOST * wide, length)
        coarse = v.astype(jnp.bfloat16)
        fine = (v - coarse.astype(jnp.float32)).astype(jnp.bfloat16)
        dot = functools.partial(jnp.dot, preferred_element_type=jnp.float32)
        moved = dot(coarse, high[i]) + dot(fine, high[i]) + dot(coarse, low[i])
        ref[pl.ds(f, count), pl.ds(target, GHOST), PAD : PAD + wide, :] = moved.reshape(
            count, GHOST, wide, length
        )

    def forward(p):
        for s in range(1, gy):
            z_landed(p, s).wait_recv()
            over_x(p, s).start()

    def finish(p):
        kept(p).wait()
        for s in range(gy):
            x_landed(p, s).wait_recv()
        move(box, 0, p, 1, GHOST + radial, 0)
        move(box, 1, p, 1, GHOST, GHOST + cells)

    build(0)
    build(1)
    forward(0)

    def piece(p, carry):
        forward(p)
        finish(p - 1)
        return carry

    build(2)
    lax.fori_loop(1, fields, piece, 0)
    finish(fields - 1)

    def sent(p, carry):
        for s in range(gy):
            over_x(p, s).wait_send()
            if s:
                over_z(p, s).wait_send()
        return carry

    lax.fori_loop(0, fields, sent, 0)

    def first(r, carry):
        for t in range(wide // 8):
            row = PAD + 8 * t
            centre, rate = tile_rates(box, r, row)
            for f in range(8):
                one[f, r, row : row + 8, :] = centre[f] + time_step * rate[f]
        return carry

    lax.fori_loop(GHOST, GHOST + cells, first, 0)

    def edge(k, carry):
        move(one, 2, 4 * k, 4, GHOST + radial - radial * x, (GHOST + cells) * x)
        return carry

    lax.fori_loop(0, fields // 4, edge, 0)

    copies = []
    for t in range(part // 8):
        row = PAD + 2 * GHOST + 8 * t

        def second(r, carry):
            at = GHOST + radial * x + r
            centre, rate = tile_rates(one, at, row)
            for f in range(8):
                start = box[f, at, row : row + 8, :]
                two[f, r, 8 * t : 8 * t + 8, :] = 0.5 * start + 0.5 * (centre[f] + time_step * rate[f])
            return carry

        lax.fori_loop(0, radial, second, 0)

        def tile(target):
            return two.at[:, :, pl.ds(8 * t, 8), pl.ds(pl.multiple_of(target * azimuth, 128), azimuth)]

        def home(source):
            return out.at[:, :, pl.ds(pl.multiple_of(source * part + 8 * t, 8), 8), :]

        for s in range(1, gy):
            back = pltpu.make_async_remote_copy(
                src_ref=tile(others[s]), dst_ref=home(me),
                send_sem=g_send.at[t, s], recv_sem=g_recv.at[t, s],
                device_id={"gy": others[s]}, device_id_type=MESH,
            )
            back.start()
            copies.append(back)
        own = pltpu.make_async_copy(tile(me), home(me), g_own.at[t])
        own.start()
        copies.append(own)
    for back in copies:
        back.wait()


def sections(rows, turned, gy, wide):
    fields, radial, tall, azimuth = turned.shape
    length, part = gy * azimuth, wide - 4 * GHOST
    padded = (fields, 2 * radial + 2 * GHOST, wide + 2 * PAD, length)
    dma = pltpu.SemaphoreType.DMA
    return pl.pallas_call(
        functools.partial(sections_kernel, gy),
        out_shape=jax.ShapeDtypeStruct((fields, radial, part * gy, azimuth), jnp.float32),
        in_specs=[pl.BlockSpec(memory_space=pltpu.VMEM), pl.BlockSpec(memory_space=pl.ANY)],
        out_specs=pl.BlockSpec(memory_space=pl.ANY),
        scratch_shapes=[
            pltpu.VMEM(padded, jnp.float32),
            pltpu.VMEM(padded, jnp.float32),
            pltpu.VMEM((fields, radial, part, length), jnp.float32),
            pltpu.VMEM((128, length), jnp.float32),
            pltpu.VMEM((3, length, length), jnp.bfloat16),
            pltpu.VMEM((3, length, length), jnp.bfloat16),
            dma((fields, gy)),
            dma((fields, gy)),
            dma((fields, gy)),
            dma((fields, gy)),
            dma((fields,)),
            dma((part // 8, gy)),
            dma((part // 8, gy)),
            dma((part // 8,)),
        ],
        compiler_params=pltpu.CompilerParams(
            collective_id=0, has_side_effects=True, vmem_limit_bytes=58 * 1024 * 1024
        ),
        name="sections",
    )(rows, turned)


def remap(cells, matrix):
    return lax.dot_general(
        cells,
        matrix,
        (((cells.ndim - 1,), (0,)), ((), ())),
        precision=lax.Precision.HIGH,
        preferred_element_type=jnp.float32,
    )


def rates(left, cells, right):
    radial, vertical = cells.shape[1], cells.shape[2] - 2 * GHOST
    inner = cells[:, :, GHOST:-GHOST]
    padded = jnp.concatenate([left, inner, right], axis=1)

    def at(f, dim, step):
        if dim == 0:
            return padded[f, GHOST + step : GHOST + step + radial]
        if dim == 2:
            return cells[f, :, GHOST + step : GHOST + step + vertical]
        return jnp.roll(inner[f], -step, axis=-1)

    def d(f, dim):
        return (8.0 * (at(f, dim, 1) - at(f, dim, -1)) - (at(f, dim, 2) - at(f, dim, -2))) / 12.0

    def second(f, dim):
        return (
            16.0 * (at(f, dim, 1) + at(f, dim, -1))
            - (at(f, dim, 2) + at(f, dim, -2))
            - 30.0 * inner[f]
        ) / 12.0

    def lap(f):
        return second(f, 0) + second(f, 1) + second(f, 2)

    return jnp.stack([
        -(d(1, 0) + d(2, 1) + d(3, 2)),
        -sound_sq * d(0, 0) + guide_field * (d(4, 2) - d(6, 0)) + 2.0 * rotation * inner[2] + viscosity * lap(1),
        -sound_sq * d(0, 1) + guide_field * (d(5, 2) - d(6, 1)) - (2.0 - shear_rate) * rotation * inner[1] + viscosity * lap(2),
        -sound_sq * d(0, 2) + viscosity * lap(3),
        guide_field * d(1, 2) - d(7, 0) + resistivity * lap(4),
        guide_field * d(2, 2) - shear_rate * rotation * inner[4] - d(7, 1) + resistivity * lap(5),
        -guide_field * (d(1, 0) + d(2, 1)) - d(7, 2) + resistivity * lap(6),
        -clean_sq * (d(4, 0) + d(5, 1) + d(6, 2)) - inner[7] / damping_time,
    ])


def around(x, axis, width, dim):
    devices, length = lax.axis_size(axis), x.shape[dim]
    up = [(i, (i + 1) % devices) for i in range(devices)]
    down = [(j, i) for i, j in up]
    before = lax.ppermute(lax.slice_in_dim(x, length - width, length, axis=dim), axis, up)
    after = lax.ppermute(lax.slice_in_dim(x, 0, width, axis=dim), axis, down)
    return before, after


def body(box_state, shear_cells, shear_fraction):
    fields, radial, azimuth, vertical = box_state.shape
    gx, gy = lax.axis_size("gx"), lax.axis_size("gy")
    length, part, wide = gy * azimuth, vertical // gy, 2 * GHOST
    at_left = lax.axis_index("gx") == 0
    at_right = lax.axis_index("gx") == gx - 1
    plus, minus = jnp.int32(1), jnp.int32(-1)

    turned = jnp.transpose(box_state, (0, 1, 3, 2))
    before, after = around(turned, "gz", wide, 2)
    turned = jnp.concatenate([before, turned, after], axis=2)
    sign = jnp.where(at_left, plus, minus)

    if gx == 2 and radial == GHOST and part % 8 == 0 and azimuth % 128 == 0:
        rows = jnp.stack([
            first_rows(8, length, shear_cells[s], shear_fraction[s], way)
            for s, way in ((0, plus), (0, minus), (1, sign))
        ])
        joined = sections(rows, turned, gy, part + 2 * wide)
        return jnp.transpose(joined, (0, 1, 3, 2))

    chunks = jnp.stack([turned[:, :, part * i : part * (i + 1) + 2 * wide] for i in range(gy)])
    landed = lax.all_to_all(chunks, "gy", split_axis=0, concat_axis=0)
    own = jnp.concatenate([landed[i] for i in range(gy)], axis=-1)

    edge = circulant(length, shear_cells[1], shear_fraction[1], sign)

    def cut(x, width):
        return x[:, :, width:-width]

    def sides(x, matrix):
        before, after = around(x, "gx", GHOST, 1)
        moved = remap(jnp.where(at_left, before, after), matrix)
        return jnp.where(at_left, moved, before), jnp.where(at_right, moved, after)

    first = circulant(length, shear_cells[0], shear_fraction[0], sign)
    raw = cut(own, GHOST)
    left, right = sides(raw, first)
    mine = raw + time_step * rates(left, own, right)
    left, right = sides(cut(mine, GHOST), edge)
    two = 0.5 * cut(own, wide) + 0.5 * (cut(mine, GHOST) + time_step * rates(left, mine, right))

    pieces = jnp.stack([two[..., azimuth * i : azimuth * (i + 1)] for i in range(gy)])
    back = lax.all_to_all(pieces, "gy", split_axis=0, concat_axis=0)
    joined = jnp.concatenate([back[i] for i in range(gy)], axis=2)
    return jnp.transpose(joined, (0, 1, 3, 2))


def solution(mesh):
    return jax.shard_map(
        body,
        mesh=mesh,
        in_specs=(P(None, "gx", ("runs", "gy"), "gz"), P("runs"), P("runs")),
        out_specs=P(None, "gx", ("runs", "gy"), "gz"),
        check_vma=False,
    )
```

profile of v0, /device:TPU:12, one launch (start us, length us, event | category | flops | bytes accessed | tf_op | source)
XLA Modules:
  0.0 154.8 jit_solution(6783269414845047995)
XLA Ops:
  0.0 0.0 copy-start
  0.0 0.0 copy-start.1
  0.0 1.9 %copy.4 = f32[8,2,256,128]{2,3,1,0:T(8,128)S(1)} copy(f32[8,2,256,128]{3,2,1,0:T(8,128)} %param.3) | data formatting | bytes 4194304 | tf_op args[0]
  2.0 0.1 collective-permute-start
  2.1 0.5 collective-permute-start.1
  2.6 0.0 copy-done
  2.6 0.6 fusion.7
  4.4 0.0 copy-done.1
  4.4 0.7 fusion.8
  9.2 1.4 divide_select_fusion.2
  10.5 0.3 divide_select_fusion
  10.9 0.7 pad_maximum_fusion.1.rows_ref
  11.5 0.0 collective-permute-done
  11.5 0.0 collective-permute-done.1
  11.5 1.6 %pad_maximum_fusion.src = f32[8,2,136,256]{3,2,1,0:T(8,128)} fusion(f32[8,2,4,256]{3,2,1,0:T(4,128)S(1)} %collective-permute-done.1, f32[8,2,128,256]{3,2,1,0:T(8,128)S(1)} %bitcast.7, f32[8,2,4,256]{3,2,1,0:T(4,128)S(1)} %collective-permute-done), kind=kLoop, calls=%fused_computation | loop fusion | flops 1114112 | bytes 4456448 | tf_op jit(solution)/shard_map/concatenate | solution.py:372
  13.2 138.7 %sections.1 = f32[8,2,128,256]{3,2,1,0:T(8,128)} custom-call(f32[3,8,1024]{2,1,0:T(8,128)} %pad_maximum_fusion.1.rows_ref, f32[8,2,136,256]{3,2,1,0:T(8,128)} %pad_maximum_fusion.src), custom_call_target="tpu_custom_call" | custom-call | tf_op jit(solution)/shard_map/sections/pallas_call | solution.py:278
  151.9 2.9 %copy.5 = f32[8,2,256,128]{3,2,1,0:T(8,128)} copy(f32[8,2,256,128]{2,3,1,0:T(8,128)} %bitcast.8) | data formatting | bytes 4194304 | tf_op jit(solution)/shard_map/transpose | solution.py:381
  (1 shorter events, 0.0 us)
Async XLA Ops:
  0.0 2.6 %copy-start = (s32[2]{0:T(128)S(1)}, s32[2]{0:T(128)}, u32[]{:S(2)}) copy-start(s32[2]{0:T(128)} %param.4) | copy-start | bytes 28
  0.0 4.4 %copy-start.1 = (f32[2]{0:T(128)S(1)}, f32[2]{0:T(128)}, u32[]{:S(2)}) copy-start(f32[2]{0:T(128)} %param.5) | copy-start | bytes 28
  2.0 9.5 %collective-permute-start = (f32[8,2,4,256]{3,2,1,0:T(4,128)S(1)}, f32[8,2,4,256]{3,2,1,0:T(4,128)S(1)}, u32[]{:S(2)}, u32[]{:S(2)}) collective-permute-start(f32[8,2,4,256]{3,2,1,0:T(4,128)S(1)} %get-tuple-element.5), channel_id=1, source_target_pairs={{0,1},{1,0},{2,3},{3,2},{4,5},{5,4},{6,7},{7,6},{8,9},{9,8},{10,11... | collective-permute-start | bytes 196616 | tf_op jit(solution)/shard_map/ppermute | solution.py:357
  2.1 9.5 %collective-permute-start.1 = (f32[8,2,4,256]{3,2,1,0:T(4,128)S(1)}, f32[8,2,4,256]{3,2,1,0:T(4,128)S(1)}, u32[]{:S(2)}, u32[]{:S(2)}) collective-permute-start(f32[8,2,4,256]{3,2,1,0:T(4,128)S(1)} %get-tuple-element.6), channel_id=1, source_target_pairs={{1,0},{0,1},{3,2},{2,3},{5,4},{4,5},{7,6},{6,7},{9,8},{8,9},{11,10... | collective-permute-start | bytes 196616 | tf_op jit(solution)/shard_map/ppermute | solution.py:358
where the time goes:
time: 156 us; the launch traced here: 155 us
  Pallas kernels  139 us (89%)
  local copies, waits for them, and re-layouts  6.09 us (4%)
  between operations  5.41 us (3%)
  other arithmetic  3.99 us (3%)
    pallas_call x1, Pallas kernels, sections(): pl.pallas_call(functools.partial(sections_kernel, gy), out_shape=jax.Shap...  139 us
  transfers between devices with their start and end apart: 2, of which 0 were waited for; matrix products, arithmetic and copies ran while one was open for 2% of the time, Pallas kernels for 0%

commit v1 on v0

--- a/solution.py
+++ b/solution.py
@@ -84,8 +84,8 @@
     ]
 
 
-def sections_kernel(gy, rows_ref, src, out, box, one, two, base, high, low,
-                    z_send, z_recv, x_send, x_recv, own_sem, g_send, g_recv, g_own):
+def sections_kernel(gy, rows_ref, state, out, src, edge_out, edge_in, box, one, two, base, high, low,
+                    z_send, z_recv, x_send, x_recv, own_sem, g_send, g_recv, g_own, e_sem):
     me, x = lax.axis_index("gy"), lax.axis_index("gx")
     fields, radial, tall, azimuth = src.shape
     cells, length = 2 * radial, gy * azimuth
@@ -102,12 +102,34 @@
         return carry
 
     lax.fori_loop(0, fields, clear, 0)
+    margin = 2 * GHOST
+    vertical = tall - 2 * margin
+
+    def turn(f, carry):
+        for r in range(radial):
+            v = jnp.transpose(state[f, r])
+            src[f, r, margin : margin + vertical, :] = v
+            edge_out[f, r, :margin, :] = v[vertical - margin :]
+            edge_out[f, r, margin:, :] = v[:margin]
+        return carry
+
+    lax.fori_loop(0, fields, turn, 0)
 
     barrier = pltpu.get_barrier_semaphore()
     for s in range(1, gy):
         pl.semaphore_signal(barrier, inc=1, device_id={"gy": others[s]}, device_id_type=MESH)
     pl.semaphore_signal(barrier, inc=1, device_id={"gx": 1 - x}, device_id_type=MESH)
-    pl.semaphore_wait(barrier, gy)
+    beside = {"gz": 1 - lax.axis_index("gz")}
+    pl.semaphore_signal(barrier, inc=1, device_id=beside, device_id_type=MESH)
+    pl.semaphore_wait(barrier, gy + 1)
+    swap = pltpu.make_async_remote_copy(
+        src_ref=edge_out, dst_ref=edge_in, send_sem=e_sem.at[0], recv_sem=e_sem.at[1],
+        device_id=beside, device_id_type=MESH,
+    )
+    swap.start()
+    swap.wait()
+    src[:, :, :margin, :] = edge_in[:, :, :margin, :]
+    src[:, :, margin + vertical :, :] = edge_in[:, :, margin:, :]
 
     def taken(p, target):
         return src.at[p, :, pl.ds(pl.multiple_of(target * part, 8), wide), :]
@@ -270,17 +292,21 @@
         back.wait()
 
 
-def sections(rows, turned, gy, wide):
-    fields, radial, tall, azimuth = turned.shape
+def sections(rows, state, gy, wide):
+    fields, radial, azimuth, vertical = state.shape
+    tall = vertical + 4 * GHOST
     length, part = gy * azimuth, wide - 4 * GHOST
     padded = (fields, 2 * radial + 2 * GHOST, wide + 2 * PAD, length)
     dma = pltpu.SemaphoreType.DMA
     return pl.pallas_call(
         functools.partial(sections_kernel, gy),
         out_shape=jax.ShapeDtypeStruct((fields, radial, part * gy, azimuth), jnp.float32),
-        in_specs=[pl.BlockSpec(memory_space=pltpu.VMEM), pl.BlockSpec(memory_space=pl.ANY)],
+        in_specs=[pl.BlockSpec(memory_space=pltpu.VMEM)] * 2,
         out_specs=pl.BlockSpec(memory_space=pl.ANY),
         scratch_shapes=[
+            pltpu.VMEM((fields, radial, tall, azimuth), jnp.float32),
+            pltpu.VMEM((fields, radial, 4 * GHOST, azimuth), jnp.float32),
+            pltpu.VMEM((fields, radial, 4 * GHOST, azimuth), jnp.float32),
             pltpu.VMEM(padded, jnp.float32),
             pltpu.VMEM(padded, jnp.float32),
             pltpu.VMEM((fields, radial, part, length), jnp.float32),
@@ -295,12 +321,13 @@
             dma((part // 8, gy)),
             dma((part // 8, gy)),
             dma((part // 8,)),
+            dma((2,)),
         ],
         compiler_params=pltpu.CompilerParams(
             collective_id=0, has_side_effects=True, vmem_limit_bytes=58 * 1024 * 1024
         ),
         name="sections",
-    )(rows, turned)
+    )(rows, state)
 
 
 def remap(cells, matrix):
@@ -367,19 +394,19 @@
     at_right = lax.axis_index("gx") == gx - 1
     plus, minus = jnp.int32(1), jnp.int32(-1)
 
-    turned = jnp.transpose(box_state, (0, 1, 3, 2))
-    before, after = around(turned, "gz", wide, 2)
-    turned = jnp.concatenate([before, turned, after], axis=2)
     sign = jnp.where(at_left, plus, minus)
 
-    if gx == 2 and radial == GHOST and part % 8 == 0 and azimuth % 128 == 0:
+    if gx == 2 and lax.axis_size("gz") == 2 and radial == GHOST and part % 8 == 0 and azimuth % 128 == 0:
         rows = jnp.stack([
             first_rows(8, length, shear_cells[s], shear_fraction[s], way)
             for s, way in ((0, plus), (0, minus), (1, sign))
         ])
-        joined = sections(rows, turned, gy, part + 2 * wide)
+        joined = sections(rows, box_state, gy, part + 2 * wide)
         return jnp.transpose(joined, (0, 1, 3, 2))
 
+    turned = jnp.transpose(box_state, (0, 1, 3, 2))
+    before, after = around(turned, "gz", wide, 2)
+    turned = jnp.concatenate([before, turned, after], axis=2)
     chunks = jnp.stack([turned[:, :, part * i : part * (i + 1) + 2 * wide] for i in range(gy)])
     landed = lax.all_to_all(chunks, "gy", split_axis=0, concat_axis=0)
     own = jnp.concatenate([landed[i] for i in range(gy)], axis=-1)

time: 156 us -> 157 us (level)
  Pallas kernels: 139 us -> 143 us
  other arithmetic: 3.99 us -> 2.42 us
    pallas_call x1, Pallas kernels: 139 us -> 143 us  [sections(): pl.pallas_call(functools.partial(sections_kernel, gy), out_shape=jax.Shap...]
    unnamed x5 -> x0, local copies, waits for them, and re-layouts: 1.95 us -> none
    concatenate x1 -> x0, other arithmetic: 1.64 us -> none  [body(): turned = jnp.concatenate([before, turned, after], axis=2)]
  transfers between devices with their start and end apart: 2 -> 0, of which waited for: 0 -> 0; matrix products, arithmetic and copies ran while one was open for 2% -> 0% of each run, Pallas kernels for 0% -> 0%
where the time goes in v1:
time: 157 us; the launch traced here: 156 us
  Pallas kernels  143 us (91%)
  local copies, waits for them, and re-layouts  5.54 us (4%)
  between operations  5.22 us (3%)
  other arithmetic  2.42 us (2%)
    pallas_call x1, Pallas kernels, sections(): pl.pallas_call(functools.partial(sections_kernel, gy), out_shape=jax.Shap...  143 us

profile of v1, /device:TPU:12, one launch (start us, length us, event | category | flops | bytes accessed | tf_op | source)
XLA Modules:
  0.0 155.9 jit_solution(11474392885966271496)
XLA Ops:
  0.0 1.3 fusion.6
  2.6 1.3 fusion.7
  7.9 1.4 divide_select_fusion.2
  9.3 0.3 divide_select_fusion
  9.6 0.7 pad_maximum_fusion.rows_ref
  10.3 142.8 %sections.1 = f32[8,2,128,256]{3,2,1,0:T(8,128)} custom-call(f32[3,8,1024]{2,1,0:T(8,128)} %pad_maximum_fusion.rows_ref, f32[8,2,256,128]{3,2,1,0:T(8,128)} %state.1), custom_call_target="tpu_custom_call" | custom-call | tf_op jit(solution)/shard_map/sections/pallas_call | solution.py:301
  153.1 2.9 %copy.4 = f32[8,2,256,128]{3,2,1,0:T(8,128)} copy(f32[8,2,256,128]{2,3,1,0:T(8,128)} %bitcast.5) | data formatting | bytes 4194304 | tf_op jit(solution)/shard_map/transpose | solution.py:405
